TPU v7x, 32 devices: a whole 2x2x4 slice. The times are simulated.
32 devices in a mesh: ctx: 16 (over z, y, core), tp: 2 (over x).
Axes of the slice: x: 2, y: 2, z: 4, core: 2. Of those that a mesh axis runs over, the one named last changes fastest.
Arguments:
- pre_queries: bfloat16 [2048, 16384], P('ctx', 'tp'), may hold values from -90 to 90
- pre_keys: bfloat16 [2048, 1024], P('ctx', 'tp'), may hold values from -4.5 to 4.5
- pre_values: bfloat16 [2048, 1024], P('ctx', 'tp'), may hold values from -6 to 6
- block_pos: int32 [32], P('ctx'), may hold values from 0 to 31, each once
- block_dest: int32 [32, 1], P('ctx'), may hold values from 0 to 15; in each aligned block of 32 rows (0 to 31, 32 to 63, ...) at most 4 rows name the same one
- dec_queries: bfloat16 [32, 4, 16384], P('ctx'), may hold values from -90 to 90
- new_keys: bfloat16 [32, 4, 1024], P('ctx', None, 'tp'), may hold values from -4.5 to 4.5
- new_values: bfloat16 [32, 4, 1024], P('ctx', None, 'tp'), may hold values from -6 to 6
- cache_keys: bfloat16 [32, 2048, 1024], P('ctx', 'tp'), may hold values from -6 to 6
- cache_values: bfloat16 [32, 2048, 1024], P('ctx', 'tp'), may hold values from -6 to 6
- cache_len: int32 [32], P('ctx'), may hold values from 1 to 2048, 32768 in all
Outputs:
- prefill_out: bfloat16 [2048, 16384], P('ctx', 'tp')
- decode_out: bfloat16 [32, 4, 16384], P('ctx', None, 'tp')
Inputs may be any that keep to these rules, and one draw needn't show every extreme that they name: `block_pos`: each of the 2 * 16 half-block positions appears once. `block_dest`: no decode index is named by more than 4 half-blocks, a bound that some block reaches. `cache_len`: some row has exactly 2048 live positions.
All inputs are finite; a program needn't handle non-finite values. No bound on the sum of `cache_len` on one device may be relied on, other than what follows from the above.
Results may differ from a plain program's by a relative error of at most 0.0065.
Values may be sent and summed in bfloat16 or wider, within the bound.
A program may use at most 192 MiB of HBM per device.

v0:
```python
import math

import jax
import jax.numpy as jnp
from jax import lax
from jax.sharding import PartitionSpec as P

QH = 128
KVH = 8
HD = 128


NEG_FILL = -1e30


def combined_all(value, axis, join):
    pieces = jax.tree.map(lambda part: lax.all_gather(part, axis), value)
    head = jax.tree.map(lambda part: part[0], pieces)
    tail = jax.tree.map(lambda part: part[1:], pieces)
    running, _ = lax.scan(lambda running, slab: (join(running, slab), None), head, tail)
    return running


def token_positions(starts, half_len):
    offsets = jnp.arange(half_len, dtype=jnp.int32)
    return (starts[:, None] * half_len + offsets[None, :]).reshape(-1)


def absorb(carry_state, scores, visible, value_block, form):
    run_peak, totals, summed = carry_state
    masked = jnp.where(visible, scores, NEG_FILL)
    new_peak = jnp.maximum(run_peak, masked.max(axis=-1))
    weights = jnp.where(visible, jnp.exp(masked - new_peak[..., None]), 0.0)
    fade_old = jnp.exp(run_peak - new_peak)
    totals = totals * fade_old + weights.sum(axis=-1)
    summed = summed * fade_old[..., None] + jnp.einsum(
        form, weights.astype(jnp.bfloat16), value_block, preferred_element_type=jnp.float32
    )
    return (new_peak, totals, summed)


def combine(left_side, right_side):
    new_peak = jnp.maximum(left_side[0], right_side[0])
    fade_left = jnp.exp(left_side[0] - new_peak)
    fade_right = jnp.exp(right_side[0] - new_peak)
    totals = left_side[1] * fade_left + right_side[1] * fade_right
    summed = left_side[2] * fade_left[..., None] + right_side[2] * fade_right[..., None]
    return (new_peak, totals, summed)


def empty_state(shape):
    return (
        jnp.full(shape, NEG_FILL, jnp.float32),
        jnp.zeros(shape, jnp.float32),
        jnp.zeros(shape + (HD,), jnp.float32),
    )


def by_turns(stacked, turn_total):
    return stacked.reshape((turn_total, stacked.shape[0] // turn_total) + stacked.shape[1:])


def per_device(
    pre_queries,
    pre_keys,
    pre_values,
    block_pos,
    block_dest,
    dec_queries,
    new_keys,
    new_values,
    cache_keys,
    cache_values,
    cache_len,
):
    tok_rows = pre_queries.shape[0]
    half_len = tok_rows // 2
    group_size = QH // KVH
    heads_dev = pre_keys.shape[1] // HD
    dec_rows = dec_queries.shape[0]
    dec_steps = dec_queries.shape[1]
    cache_dev = cache_keys.shape[1]
    inv_root = 1.0 / math.sqrt(HD)
    tp_index = lax.axis_index("tp")
    ctx_index = lax.axis_index("ctx")
    queries = pre_queries.reshape(tok_rows, heads_dev, group_size, HD)
    query_pos = token_positions(block_pos, half_len)
    own_width = heads_dev * group_size * HD
    own_queries = lax.dynamic_slice_in_dim(dec_queries, tp_index * own_width, own_width, 2).reshape(
        dec_rows, dec_steps, heads_dev, group_size, HD
    )

    def turn_count(shards):
        shard_count = shards.shape[0] // tok_rows
        return shard_count // math.gcd(shard_count, max(1, 1024 // tok_rows))

    def prefill_turn(carry_state, key_block, value_block, starts):
        key_block = key_block.reshape(-1, heads_dev, HD)
        value_block = value_block.reshape(-1, heads_dev, HD)
        key_pos = token_positions(starts, half_len)
        scores = (
            jnp.einsum("tkgd,ukd->tkgu", queries, key_block, preferred_element_type=jnp.float32)
            * inv_root
        )
        visible = (key_pos[None, :] <= query_pos[:, None])[:, None, None, :]
        return absorb(carry_state, scores, visible, value_block, "tkgu,ukd->tkgd")

    def decode_turn(carry_state, key_block, value_block, owners):
        key_block = key_block.reshape(-1, heads_dev, HD)
        value_block = value_block.reshape(-1, heads_dev, HD)
        scores = (
            jnp.einsum(
                "rskgd,ukd->rskgu", own_queries, key_block, preferred_element_type=jnp.float32
            )
            * inv_root
        )
        visible = jnp.repeat(owners[:, 0], half_len) == ctx_index
        return absorb(carry_state, scores, visible, value_block, "rskgu,ukd->rskgd")

    prefill_start = empty_state((tok_rows, heads_dev, group_size))
    decode_start = empty_state((dec_rows, dec_steps, heads_dev, group_size))
    shards = (
        lax.all_gather(pre_keys, "ctx", axis=0, tiled=True),
        lax.all_gather(pre_values, "ctx", axis=0, tiled=True),
        lax.all_gather(block_pos, "ctx", axis=0, tiled=True),
    )
    turn_total = turn_count(shards[0])

    def one_turn(inner, member):
        return (prefill_turn(inner, member[0], member[1], member[2]), None)

    result, _ = lax.scan(
        one_turn, prefill_start, tuple((by_turns(stacked, turn_total) for stacked in shards))
    )
    shards = (
        lax.all_gather(pre_keys, "ctx", axis=0, tiled=True),
        lax.all_gather(pre_values, "ctx", axis=0, tiled=True),
        lax.all_gather(block_dest, "ctx", axis=0, tiled=True),
    )
    turn_total = turn_count(shards[0])

    def one_turn(inner, member):
        return (decode_turn(inner, member[0], member[1], member[2]), None)

    fold_result, _ = lax.scan(
        one_turn, decode_start, tuple((by_turns(stacked, turn_total) for stacked in shards))
    )
    prefill_out = (
        (result[2] / result[1][..., None]).reshape(tok_rows, own_width).astype(jnp.bfloat16)
    )
    fresh_keys = new_keys.reshape(dec_rows, dec_steps, heads_dev, HD)
    fresh_values = new_values.reshape(dec_rows, dec_steps, heads_dev, HD)
    step_order = jnp.arange(dec_steps, dtype=jnp.int32)
    scores = (
        jnp.einsum("rskgd,rukd->rskgu", own_queries, fresh_keys, preferred_element_type=jnp.float32)
        * inv_root
    )
    visible = (step_order[None, :] <= step_order[:, None])[None, :, None, None, :]
    own_state = absorb(fold_result, scores, visible, fresh_values, "rskgu,rukd->rskgd")
    all_queries = dec_queries.reshape(dec_rows, dec_steps, KVH, group_size, HD)
    stored_keys = cache_keys.reshape(dec_rows, cache_dev, KVH, HD)
    stored_values = cache_values.reshape(dec_rows, cache_dev, KVH, HD)
    scores = (
        jnp.einsum(
            "rskgd,rukd->rskgu", all_queries, stored_keys, preferred_element_type=jnp.float32
        )
        * inv_root
    )
    cache_pos = tp_index * cache_dev + jnp.arange(cache_dev, dtype=jnp.int32)
    visible = (cache_pos[None, :] < cache_len[:, None])[:, None, None, None, :]
    cache_state = absorb(
        empty_state((dec_rows, dec_steps, KVH, group_size)),
        scores,
        visible,
        stored_values,
        "rskgu,rukd->rskgd",
    )
    blank_state = empty_state((dec_rows, dec_steps, KVH, group_size))
    placed = tuple(
        (
            lax.dynamic_update_slice_in_dim(full_part, own_part, tp_index * heads_dev, 2)
            for full_part, own_part in zip(blank_state, own_state)
        )
    )
    run_peak, totals, summed = combine(cache_state, placed)
    run_peak, totals, summed = combined_all((run_peak, totals, summed), "tp", combine)
    totals = lax.dynamic_slice_in_dim(totals, tp_index * heads_dev, heads_dev, 2)
    summed = lax.dynamic_slice_in_dim(summed, tp_index * heads_dev, heads_dev, 2)
    decode_out = (
        (summed / totals[..., None]).reshape(dec_rows, dec_steps, own_width).astype(jnp.bfloat16)
    )
    return (prefill_out, decode_out)


def solution(mesh):
    placed = (
        P("ctx", "tp"),
        P("ctx", "tp"),
        P("ctx", "tp"),
        P("ctx"),
        P("ctx", None),
        P("ctx", None, None),
        P("ctx", None, "tp"),
        P("ctx", None, "tp"),
        P("ctx", "tp", None),
        P("ctx", "tp", None),
        P("ctx"),
    )
    return jax.shard_map(
        per_device,
        mesh=mesh,
        in_specs=placed,
        out_specs=(P("ctx", "tp"), P("ctx", None, "tp")),
        check_vma=False,
    )
```

profile of v0, /device:TPU:0, one launch (start us, length us, event | category | flops | bytes accessed | tf_op | source)
XLA Modules:
  0.0 251.8 jit_solution(9705565003066734000)
XLA Ops:
  7.2 0.7 all-gather.7.cloned.1.call-update
  8.0 0.7 all-gather.9.cloned.1.call-update
  8.8 1.2 dynamic-slice
  10.7 0.9 dynamic-update-slice
  11.5 0.7 bitcast_dynamic-update-slice_fusion
  12.3 13.7 %all-reduce.2 = (s32[32]{0:T(128)S(1)}, s32[32]{0:T(128)S(1)}) all-reduce(s32[32]{0:T(128)S(1)} %dynamic-update-slice, s32[32]{0:T(128)S(1)} %bitcast_dynamic-update-slice_fusion), channel_id=1, replica_groups=mesh['ctx'=16,'tp'=2] {'ctx'}, use_global_device_ids=true, to_apply=%add | all-reduce | flops 64 | bytes 512
  26.1 3.2 %copy.108 = bf16[128,8192]{0,1:T(8,128)(2,1)S(1)} copy(bf16[128,8192]{1,0:T(8,128)(2,1)} %param.15) | data formatting | bytes 4194304 | tf_op args[0]
  29.3 2.6 %copy.110 = bf16[128,4,16,128]{3,0,2,1:T(8,128)(2,1)} copy(bf16[128,4,16,128]{0,3,2,1:T(8,128)(2,1)S(1)} %bitcast.186) | data formatting | bytes 4194304
  31.9 5.3 %copy.151 = bf16[256,8,8,128]{3,2,1,0:T(8,128)(2,1)} copy(bf16[256,8,8,128]{3,1,2,0:T(8,128)(2,1)} %bitcast.187) | data formatting | bytes 8388608
  37.6 5.2 %copy.150 = bf16[256,8,8,128]{3,2,1,0:T(8,128)(2,1)} copy(bf16[256,8,8,128]{3,1,2,0:T(8,128)(2,1)} %bitcast.188) | data formatting | bytes 8388608
  42.8 0.6 reshape.206
  43.6 0.7 copy.118
  44.4 2.5 bitcast_bitcast_fusion.1
  46.9 1.8 bitcast_reduce_fusion.1
  48.8 1.6 fusion.96
  50.9 1.8 fusion.38
  52.7 2.3 bitcast_bitcast_fusion
  55.0 3.0 %copy.109 = bf16[2,1024,512]{1,2,0:T(8,128)(2,1)S(1)} copy(bf16[2,1024,512]{2,1,0:T(8,128)(2,1)} %bitcast.189) | data formatting | bytes 4194304
  58.0 38.6 %all-gather.9.cloned.1.call-done = bf16[2048,512]{1,0:T(8,128)(2,1)} async-done(((bf16[128,512]{1,0:T(8,128)(2,1)}), bf16[2048,512]{1,0:T(8,128)(2,1)}) %all-gather.9.cloned.1.call-update) | async-done | bytes 2097168 | tf_op jit(solution)/shard_map/all_gather | solution.py:124
  96.6 4.0 %copy.111 = bf16[2,1024,512]{1,2,0:T(8,128)(2,1)} copy(bf16[2,1024,512]{2,1,0:T(8,128)(2,1)} %bitcast.190) | data formatting | bytes 4194304
  100.6 95.1 %while.36 = (s32[]{:T(128)}, f32[128,4,16]{0,2,1:T(8,128)S(1)}, f32[128,4,16]{0,2,1:T(8,128)S(1)}, f32[128,4,16,128]{0,3,2,1:T(8,128)}, s32[2,16]{1,0:T(2,128)S(...) while((s32[]{:T(128)}, f32[128,4,16]{0,2,1:T(8,128)S(1)}, ...), condition=%wide.region_3.4_spmd.clone, body=%wide.region_0.3_spmd.clone.sunk | while | flops 4407337984 | bytes 126896488 | solution.py:132
  101.3 1.6 constant_dynamic-slice_fusion.11
  103.0 13.4 %fusion.123 = (f32[128,4,16]{0,2,1:T(8,128)S(1)}, f32[4,1024,128,16]{2,1,3,0:T(8,128)}) fusion(pred[128,1024]{0,1:T(8,128)(4,1)S(1)} %broadcast_compare_fusion.3, bf16[1024,4,128,1]{0,2,3,1:T(8,128)(2,1)S(1)} %bitcast.179, bf16[128,4,16,128]{3,0,2,1:T(8,128)(2,1)S(1)} %copy-done.1), kind=kOutput, calls=%fused_computation.3.clone.1 | convolution fusion | flops 2172641280 | bytes 36864000 | tf_op jit(solution)/shard_map/while/body/eval_jaxpr/tkgd,ukd->tkgu/dot_general | solution.py:102
  116.3 15.0 %fusion.124 = f32[128,4,16]{0,2,1:T(8,128)S(1)} fusion(f32[4,1024,128,16]{2,1,3,0:T(8,128)} %get-tuple-element.465, f32[128,4,16]{0,2,1:T(8,128)S(1)} %select_maximum_fusion.4, pred[128,1024]{0,1:T(8,128)(4,1)S(1)} %broadcast_compare_fusion.3), kind=kLoop, calls=%fused_computation.5.clone.1 | loop fusion | flops 41934848 | bytes 33751040 | tf_op jit(solution)/shard_map/while/body/eval_jaxpr/reduce_sum | solution.py:35
  131.4 16.1 %bitcast_add_fusion.2 = f32[128,4,16,128]{0,3,2,1:T(8,128)} fusion(f32[128,4,16,128]{0,3,2,1:T(8,128)} %get-tuple-element.498, bf16[1024,4,128,1]{0,2,3,1:T(8,128)(2,1)S(1)} %bitcast.180, f32[4,1024,128,16]{2,1,3,0:T(8,128)} %get-tuple-element.465, f32[128,4,16]{0,2,1:T(8,128)S(1)} %select_maximum_fusion.4, ...), kind=kOutput, calls=%fused_computation.8.clone.1 | convolution fusion | flops 2192572416 | bytes 43188224 | tf_op jit(solution)/shard_map/while/body/eval_jaxpr/tkgu,ukd->tkgd/dot_general | solution.py:36
  148.0 1.6 constant_dynamic-slice_fusion.11
  149.7 13.4 %fusion.123 = (f32[128,4,16]{0,2,1:T(8,128)S(1)}, f32[4,1024,128,16]{2,1,3,0:T(8,128)}) fusion(pred[128,1024]{0,1:T(8,128)(4,1)S(1)} %broadcast_compare_fusion.3, bf16[1024,4,128,1]{0,2,3,1:T(8,128)(2,1)S(1)} %bitcast.179, bf16[128,4,16,128]{3,0,2,1:T(8,128)(2,1)S(1)} %copy-done.1), kind=kOutput, calls=%fused_computation.3.clone.1 | convolution fusion | flops 2172641280 | bytes 36864000 | tf_op jit(solution)/shard_map/while/body/eval_jaxpr/tkgd,ukd->tkgu/dot_general | solution.py:102
  163.1 15.0 %fusion.124 = f32[128,4,16]{0,2,1:T(8,128)S(1)} fusion(f32[4,1024,128,16]{2,1,3,0:T(8,128)} %get-tuple-element.465, f32[128,4,16]{0,2,1:T(8,128)S(1)} %select_maximum_fusion.4, pred[128,1024]{0,1:T(8,128)(4,1)S(1)} %broadcast_compare_fusion.3), kind=kLoop, calls=%fused_computation.5.clone.1 | loop fusion | flops 41934848 | bytes 33751040 | tf_op jit(solution)/shard_map/while/body/eval_jaxpr/reduce_sum | solution.py:35
  178.1 17.6 %bitcast_add_fusion.2 = f32[128,4,16,128]{0,3,2,1:T(8,128)} fusion(f32[128,4,16,128]{0,3,2,1:T(8,128)} %get-tuple-element.498, bf16[1024,4,128,1]{0,2,3,1:T(8,128)(2,1)S(1)} %bitcast.180, f32[4,1024,128,16]{2,1,3,0:T(8,128)} %get-tuple-element.465, f32[128,4,16]{0,2,1:T(8,128)S(1)} %select_maximum_fusion.4, ...), kind=kOutput, calls=%fused_computation.8.clone.1 | convolution fusion | flops 2192572416 | bytes 43188224 | tf_op jit(solution)/shard_map/while/body/eval_jaxpr/tkgu,ukd->tkgd/dot_general | solution.py:36
  195.8 17.6 %while.37 = (s32[]{:T(128)}, f32[2,4,4,16]{3,1,0,2:T(4,128)S(1)}, f32[2,4,4,16]{3,1,0,2:T(4,128)S(1)}, f32[2,4,4,16,128]{4,3,1,0,2:T(8,128)}, s32[2,16,1]{1,2,0:...) while((s32[]{:T(128)}, f32[2,4,4,16]{3,1,0,2:T(4,128)S(1)}, ...), condition=%wide.region_8.9_spmd.clone, body=%wide.region_5.8_spmd.clone.sunk | while | flops 275450368 | bytes 13801737 | solution.py:145
  196.0 1.5 constant_dynamic-slice_fusion.12
  197.5 1.8 bitcast_reduce_fusion.3
  199.3 2.2 fusion.130
  201.5 3.0 %fusion.132 = f32[2,4,4,16,128]{4,3,1,0,2:T(8,128)} fusion(bf16[1024,4,128,1,1]{0,2,4,3,1:T(8,128)(2,1)S(1)} %bitcast.181, f32[4,1024,2,4,16]{1,4,3,2,0:T(8,128)} %get-tuple-element.480, f32[2,4,4,16]{3,1,0,2:T(4,128)S(1)} %select_maximum_fusion.5, pred[1024]{0:T(1024)(128)(4,1)S(1)} %eq.24, f32[2,4,4,16,128]{4,3,1,0,2:T(8,128)} %get-tuple-element.531, ...), kind=kOutput, calls=%fused_computation.33.clone.1 | convolution fusion | flops 137035776 | bytes 3675137 | tf_op jit(solution)/shard_map/while/body/eval_jaxpr/rskgu,ukd->rskgd/dot_general | solution.py:36
  204.7 1.5 constant_dynamic-slice_fusion.12
  206.3 1.8 bitcast_reduce_fusion.3
  208.1 2.2 fusion.130
  210.3 3.0 %fusion.132 = f32[2,4,4,16,128]{4,3,1,0,2:T(8,128)} fusion(bf16[1024,4,128,1,1]{0,2,4,3,1:T(8,128)(2,1)S(1)} %bitcast.181, f32[4,1024,2,4,16]{1,4,3,2,0:T(8,128)} %get-tuple-element.480, f32[2,4,4,16]{3,1,0,2:T(4,128)S(1)} %select_maximum_fusion.5, pred[1024]{0:T(1024)(128)(4,1)S(1)} %eq.24, f32[2,4,4,16,128]{4,3,1,0,2:T(8,128)} %get-tuple-element.531, ...), kind=kOutput, calls=%fused_computation.33.clone.1 | convolution fusion | flops 137035776 | bytes 3675137 | tf_op jit(solution)/shard_map/while/body/eval_jaxpr/rskgu,ukd->rskgd/dot_general | solution.py:36
  213.7 1.4 fusion.68
  215.1 5.4 %fusion.62 = f32[2,4,8,16,128]{4,3,1,2,0:T(8,128)S(1)} fusion(bf16[2,1024,8,128,1]{3,2,1,0,4:T(8,128)(2,1)} %bitcast_bitcast_fusion, f32[2,8,1024,4,16]{2,4,3,1,0:T(8,128)} %copy-done.3, f32[2,4,8,16]{3,1,2,0:T(4,128)S(1)} %copy-done.10, pred[2,1024]{1,0:T(4,128)(4,1)S(1)} %copy-done.15, f32[2,4,8,16,128]{4,3,1,2,0:T(8,128)S(1)} %fusion.68, ...), kind=kOutput, calls=%fused_computation.75 | convolution fusion | flops 274202624 | bytes 9455616 | tf_op jit(solution)/shard_map/rskgu,rukd->rskgd/dot_general | solution.py:36
  220.5 0.9 copy.126
  221.4 2.8 %divide_convert_fusion = bf16[128,4,16,128]{0,3,2,1:T(8,128)(2,1)S(1)} fusion(f32[128,4,16,128]{0,3,2,1:T(8,128)} %get-tuple-element.120, f32[128,4,16]{0,2,1:T(8,128)S(1)} %get-tuple-element.121), kind=kLoop, calls=%fused_computation.63 | loop fusion | flops 2097152 | bytes 6324224 | tf_op jit(solution)/shard_map/convert_element_type | solution.py:149
  224.2 2.9 %copy.139 = bf16[128,8192]{1,0:T(8,128)(2,1)} copy(bf16[128,8192]{0,1:T(8,128)(2,1)S(1)} %bitcast.185) | data formatting | bytes 4194304 | tf_op jit(solution)/shard_map/convert_element_type | solution.py:149
  227.1 5.1 %all-gather.2 = f32[4,4,8,16]{3,2,1,0:T(8,128)S(1)} all-gather(f32[2,4,8,16]{3,2,1,0:T(8,128)S(1)} %copy.129), channel_id=4, replica_groups=mesh['ctx'=16,'tp'=2] {'tp'}, dimensions={0}, use_global_device_ids=true | all-gather | bytes 12288 | tf_op jit(solution)/shard_map/all_gather | solution.py:17
  232.1 5.2 %all-gather.1 = f32[4,4,8,16]{3,2,1,0:T(8,128)S(1)} all-gather(f32[2,4,8,16]{3,2,1,0:T(8,128)S(1)} %copy.127), channel_id=3, replica_groups=mesh['ctx'=16,'tp'=2] {'tp'}, dimensions={0}, use_global_device_ids=true | all-gather | bytes 12288 | tf_op jit(solution)/shard_map/all_gather | solution.py:17
  237.4 5.6 %all-gather.11.cloned.1.call-done = f32[4,4,8,16,128]{4,3,2,1,0:T(8,128)} async-done(((f32[2,4,8,16,128]{4,3,2,1,0:T(8,128)}), f32[4,4,8,16,128]{4,3,2,1,0:T(8,128)}) %all-gather.11.cloned.1.call-update) | async-done | bytes 1048592 | tf_op jit(solution)/shard_map/all_gather | solution.py:17
  243.0 1.3 fusion.94
  244.6 0.7 convert_element_type.29
  (115 shorter events, 3.7 us)
Async XLA Ops:
  7.2 206.5 %copy-start = (bf16[2,4,512]{2,1,0:T(4,128)(2,1)S(1)}, bf16[2,4,512]{2,1,0:T(4,128)(2,1)}, u32[]{:S(2)}) copy-start(bf16[2,4,512]{2,1,0:T(4,128)(2,1)} %param.22) | copy-start | bytes 24580
  7.2 47.8 %all-gather.7.cloned.1.call-start = ((), (), s32[]{:S(2)}) async-start(), calls=%async_computation | async-start | bytes 2228224 | tf_op jit(solution)/shard_map/all_gather | solution.py:123
  7.9 88.7 %all-gather.9.cloned.1.call-start = ((), (), s32[]{:S(2)}) async-start(), calls=%async_computation.1 | async-start | bytes 2228224 | tf_op jit(solution)/shard_map/all_gather | solution.py:124
  8.7 234.3 %all-gather.11.cloned.1.call-start = ((), (), s32[]{:S(2)}) async-start(), calls=%async_computation.2 | async-start | bytes 1572864 | tf_op jit(solution)/shard_map/all_gather | solution.py:17
  31.9 5.3 %copy-start.5 = (bf16[2,4,16384]{2,1,0:T(4,128)(2,1)S(1)}, bf16[2,4,16384]{2,1,0:T(4,128)(2,1)}, u32[]{:S(2)}) copy-start(bf16[2,4,16384]{2,1,0:T(4,128)(2,1)} %param.20) | copy-start | bytes 786436
  37.5 6.8 %copy-start.22 = (s32[2]{0:T(128)S(1)}, s32[2]{0:T(128)}, u32[]{:S(2)}) copy-start(s32[2]{0:T(128)} %param.18) | copy-start | bytes 28
  37.5 6.8 %copy-start.20 = (s32[2]{0:T(128)S(1)}, s32[2]{0:T(128)}, u32[]{:S(2)}) copy-start(s32[2]{0:T(128)} %param.25) | copy-start | bytes 28
  44.3 4.5 %copy-start.18 = (pred[4,4]{1,0:T(4,128)(4,1)}, pred[4,4]{1,0:T(4,128)(4,1)S(1)}, u32[]{:S(2)}) copy-start(pred[4,4]{1,0:T(4,128)(4,1)S(1)} %iota_compare_fusion) | copy-start | bytes 52
  44.4 6.0 %copy-start.14 = (pred[2,1024]{1,0:T(4,128)(4,1)}, pred[2,1024]{1,0:T(4,128)(4,1)S(1)}, u32[]{:S(2)}) copy-start(pred[2,1024]{1,0:T(4,128)(4,1)S(1)} %broadcast_compare_fusion.1) | copy-start | bytes 6148
  46.9 1.9 copy-start.21
  48.7 2.2 copy-start.3
  48.7 6.3 %copy-start.11 = (f32[2,4,8,16]{3,1,2,0:T(4,128)}, f32[2,4,8,16]{3,1,2,0:T(4,128)S(1)}, u32[]{:S(2)}) copy-start(f32[2,4,8,16]{3,1,2,0:T(4,128)S(1)} %get-tuple-element.346) | copy-start | bytes 12292
  48.7 4.0 %copy-start.2 = (bf16[256,8,8,128]{3,2,1,0:T(8,128)(2,1)S(1)}, bf16[256,8,8,128]{3,2,1,0:T(8,128)(2,1)}, u32[]{:S(2)}) copy-start(bf16[256,8,8,128]{3,2,1,0:T(8,128)(2,1)} %copy.151) | copy-start | bytes 12582916
  48.8 6.2 %copy-start.9 = (f32[2,4,8,16]{3,1,2,0:T(4,128)}, f32[2,4,8,16]{3,1,2,0:T(4,128)S(1)}, u32[]{:S(2)}) copy-start(f32[2,4,8,16]{3,1,2,0:T(4,128)S(1)} %broadcast_maximum_fusion) | copy-start | bytes 12292
  100.6 95.1 %copy-start.4 = (f32[2,4,4,16]{3,1,0,2:T(4,128)S(1)}, f32[2,4,4,16]{3,1,0,2:T(4,128)}, u32[]{:S(2)}) copy-start(f32[2,4,4,16]{3,1,0,2:T(4,128)} %custom-call.3) | copy-start | bytes 6148
  100.6 95.1 %copy-start.6 = (f32[2,4,4,16]{3,1,0,2:T(4,128)S(1)}, f32[2,4,4,16]{3,1,0,2:T(4,128)}, u32[]{:S(2)}) copy-start(f32[2,4,4,16]{3,1,0,2:T(4,128)} %custom-call.4) | copy-start | bytes 6148
  100.6 95.1 %copy-start.17 = (s32[2,16,1]{1,0,2:T(2,128)S(1)}, s32[2,16,1]{1,0,2:T(2,128)}, u32[]{:S(2)}) copy-start(s32[2,16,1]{1,0,2:T(2,128)} %reshape.206) | copy-start | bytes 388
  101.1 1.9 copy-start.1
  147.8 1.9 copy-start.1
  195.7 17.6 %copy-start.16 = (f32[2,4,4,16]{3,1,2,0:T(4,128)S(1)}, f32[2,4,4,16]{3,1,2,0:T(4,128)}, u32[]{:S(2)}) copy-start(f32[2,4,4,16]{3,1,2,0:T(4,128)} %get-tuple-element.348) | copy-start | bytes 6148
  195.7 17.6 %copy-start.7 = (f32[2,4,4,16,4]{3,4,1,2,0:T(4,128)S(1)}, f32[2,4,4,16,4]{3,4,1,2,0:T(4,128)}, u32[]{:S(2)}) copy-start(f32[2,4,4,16,4]{3,4,1,2,0:T(4,128)} %get-tuple-element.349) | copy-start | bytes 24580
  195.7 17.6 %copy-start.19 = (pred[4,4]{1,0:T(4,128)(4,1)S(1)}, pred[4,4]{1,0:T(4,128)(4,1)}, u32[]{:S(2)}) copy-start(pred[4,4]{1,0:T(4,128)(4,1)} %copy-done.18) | copy-start | bytes 52
  195.7 17.8 %copy-start.8 = (f32[2,4,8,16]{3,1,2,0:T(4,128)S(1)}, f32[2,4,8,16]{3,1,2,0:T(4,128)}, u32[]{:S(2)}) copy-start(f32[2,4,8,16]{3,1,2,0:T(4,128)} %fusion.38) | copy-start | bytes 12292
  195.7 17.8 %copy-start.12 = (f32[2,4,8,16]{3,1,2,0:T(4,128)S(1)}, f32[2,4,8,16]{3,1,2,0:T(4,128)}, u32[]{:S(2)}) copy-start(f32[2,4,8,16]{3,1,2,0:T(4,128)} %copy-done.11) | copy-start | bytes 12292
  195.7 19.3 %copy-start.10 = (f32[2,4,8,16]{3,1,2,0:T(4,128)S(1)}, f32[2,4,8,16]{3,1,2,0:T(4,128)}, u32[]{:S(2)}) copy-start(f32[2,4,8,16]{3,1,2,0:T(4,128)} %copy-done.9) | copy-start | bytes 12292
  195.8 19.3 %copy-start.15 = (pred[2,1024]{1,0:T(4,128)(4,1)S(1)}, pred[2,1024]{1,0:T(4,128)(4,1)}, u32[]{:S(2)}) copy-start(pred[2,1024]{1,0:T(4,128)(4,1)} %copy-done.14) | copy-start | bytes 6148
  196.0 1.5 copy-start.13
  204.7 1.5 copy-start.13
Sparse Core Ops, SparseCore 0:
  10.2 44.0 all-gather.6
  56.4 40.1 all-gather.8
  221.5 21.4 all-gather.10
where the time goes:
time: 253 us; the launch traced here: 252 us
  matrix products  80.2 us (32%)
  local copies, waits for them, and re-layouts  46.2 us (18%)
  waiting for transfers between devices  45.6 us (18%)
  other arithmetic  40.4 us (16%)
  blocking collectives  24 us (9%)
  between operations  14.8 us (6%)
    dot_general x6, matrix products, absorb(): jnp.einsum(form, weights.astype(jnp.bfloat16), value_block, preferred_ele...  46.5 us
    all_gather x1, waiting for transfers between devices, per_device(): lax.all_gather(pre_values, 'ctx', axis=0, tiled=True)  38.6 us
    reduce_sum x6, other arithmetic, absorb(): totals = totals * fade_old + weights.sum(axis=-1)  36.3 us
    unnamed x54, local copies, waits for them, and re-layouts  27.4 us
    dot_general x2, matrix products, prefill_turn(): jnp.einsum('tkgd,ukd->tkgu', queries, key_block, preferred_element_type=j...  26.7 us
    unnamed x1, blocking collectives  13.7 us
    all_gather x2, blocking collectives, combined_all(): pieces = jax.tree.map(lambda part: lax.all_gather(part, axis), value)  10.3 us
    dynamic_slice x4, local copies, waits for them, and re-layouts, per_device(): lax.scan(one_turn, prefill_start, tuple((by_turns(stacked, turn_total) fo...  6.27 us
  transfers between devices with their start and end apart: 3, of which 2 were waited for; matrix products, arithmetic and copies ran while one was open for 16% of the time, Pallas kernels for 0%

commit v1 on v0

v1 whole, which is shorter than its diff:
```python
import functools
import math

import jax
import jax.numpy as jnp
from jax import lax
from jax.experimental import pallas as pl
from jax.experimental.pallas import tpu as pltpu
from jax.sharding import PartitionSpec as P

QH = 128
KVH = 8
HD = 128
GROUP = QH // KVH
FILL = -1e30
C2 = math.log2(math.e) / math.sqrt(HD)
META = 16
HEADS_STEP = 4
NT = (((1,), (1,)), ((), ()))


def lanes(index, width=HD):
    return pl.ds(pl.multiple_of(index * width, HD), width)


def softmax_tile(scores, bias, old):
    width = scores.shape[1] // HD
    parts = [scores[:, c * HD : (c + 1) * HD] * C2 + bias(c) for c in range(width)]
    top = functools.reduce(jnp.maximum, parts)
    peak = jnp.broadcast_to(jnp.max(top, axis=-1, keepdims=True), top.shape)
    fade = None
    if old is not None:
        peak = jnp.maximum(peak, old)
        fade = jnp.exp2(old - peak)
    parts = [jnp.exp2(part - peak) for part in parts]
    total = functools.reduce(jnp.add, parts)
    weights = jnp.concatenate([part.astype(jnp.bfloat16) for part in parts], axis=1)
    return peak, fade, total, weights


def kernel(
    n_ctx,
    n_tp,
    pos_ref,
    len_ref,
    load_ref,
    q_ref,
    dq_ref,
    fresh_ref,
    ck_hbm,
    cv_hbm,
    out_ref,
    dec_ref,
    slots,
    peak_ref,
    total_ref,
    acc_ref,
    bias_ref,
    dbias_ref,
    ck,
    cv,
    cst,
    rx,
    ring_send,
    ring_recv,
    sib_send,
    sib_recv,
    tp_send,
    tp_recv,
    cache_sem,
):
    tok = q_ref.shape[0]
    half_len = tok // 2
    hd = load_ref.shape[1] // HD
    heads = hd * GROUP
    rows = ck.shape[0]
    cache_dev = ck.shape[1]
    per_row = dq_ref.shape[1] // rows
    n_chip = n_ctx // 2
    half = n_chip // 2

    me = lax.axis_index("ctx")
    tp = lax.axis_index("tp")
    chip, core = lax.div(me, 2), lax.rem(me, 2)
    sibling = me + 1 - 2 * core
    line, along = lax.rem(chip, 2), lax.div(chip, 2)
    place = along + line * (n_chip - 1 - 2 * along)

    def chip_at(position):
        position = lax.rem(position + 2 * n_chip, n_chip)
        far = lax.div(position, half)
        return 2 * (position + far * (n_chip - 1 - 2 * position)) + far

    def owner(position):
        return chip_at(position) * 2 + core

    def sib_owner(position):
        return chip_at(position) * 2 + 1 - core

    right, left = owner(place + 1), owner(place - 1)

    cache_copies = []
    for r in range(rows):
        pair = []
        for which, (src, dst) in enumerate(((ck_hbm, ck), (cv_hbm, cv))):
            copy = pltpu.make_async_copy(src.at[r], dst.at[r], cache_sem.at[r, which])
            copy.start()
            pair.append(copy)
        cache_copies.append(pair)

    barrier = pltpu.get_barrier_semaphore()
    for other in (right, left, sibling):
        pl.semaphore_signal(
            barrier, inc=1, device_id={"ctx": other}, device_id_type=pl.DeviceIdType.MESH
        )
    for d in range(1, n_tp):
        pl.semaphore_signal(
            barrier,
            inc=1,
            device_id={"tp": lax.rem(tp + d, n_tp)},
            device_id_type=pl.DeviceIdType.MESH,
        )
    pl.semaphore_wait(barrier, 3 + n_tp - 1)

    def ring_copy(way, step, src, slot, part):
        dst = slots.at[slot] if part is None else slots.at[slot, part]
        return pltpu.make_async_remote_copy(
            src_ref=dst if src is None else src,
            dst_ref=dst,
            send_sem=ring_send.at[way, step],
            recv_sem=ring_recv.at[way, step],
            device_id={"ctx": left if way else right},
            device_id_type=pl.DeviceIdType.MESH,
        )

    def sib_copy(way, step, src, slot):
        dst = slots.at[slot]
        return pltpu.make_async_remote_copy(
            src_ref=dst if src is None else src,
            dst_ref=dst,
            send_sem=sib_send.at[way, step],
            recv_sem=sib_recv.at[way, step],
            device_id={"ctx": sibling},
            device_id_type=pl.DeviceIdType.MESH,
        )

    first_part, second_part = pl.ds(0, tok + META), pl.ds(tok + META, tok)
    sent = []

    def start(copy):
        copy.start()
        sent.append(copy)

    def part_of(way, step):
        if step < half:
            return None
        return second_part if way else first_part

    start(ring_copy(0, 1, load_ref, me, None))
    start(ring_copy(1, 1, load_ref, me, None))
    start(sib_copy(0, 0, load_ref, me))

    def ring_arrive(step):
        slot = [owner(place - step), owner(place + step)]
        for way in (0, 1):
            ring_copy(way, step, None, slot[way], part_of(way, step)).wait_recv()
            if step < half:
                start(ring_copy(way, step + 1, None, slot[way], part_of(way, step + 1)))
        if step < half:
            start(sib_copy(0, step, None, slot[0]))
            start(sib_copy(1, step, None, slot[1]))
            return [slots.at[slot[0]], slots.at[slot[1]]]
        start(sib_copy(0, step, None, slot[0]))
        return [slots.at[slot[0]]]

    def sib_arrive(step):
        slot = [sib_owner(place - step), sib_owner(place + step)]
        ways = (0, 1) if 0 < step < half else (0,)
        for way in ways:
            sib_copy(way, step, None, slot[way]).wait_recv()
        return [slots.at[slot[way]] for way in ways]

    row = lax.broadcasted_iota(jnp.int32, (tok, HD), 0)
    lane = lax.broadcasted_iota(jnp.int32, (tok, HD), 1)
    own_pos = jnp.where(row < half_len, pos_ref[0], pos_ref[1]) * half_len + lax.rem(row, half_len)
    own_pos = own_pos.astype(jnp.float32)
    lane_off = lax.rem(lane, half_len).astype(jnp.float32)
    me_f = me.astype(jnp.float32)

    def chunk(blocks, first, last):
        width = len(blocks)
        for c, block in enumerate(blocks):
            meta = block[tok : tok + META, 0:HD].astype(jnp.float32)
            key_pos = meta[0:1, :] * float(half_len) + lane_off
            bias_ref[c] = jnp.where(key_pos <= own_pos, 0.0, FILL)
            dbias_ref[c] = jnp.where(jnp.broadcast_to(meta[1:2, :], (tok, HD)) == me_f, 0.0, FILL)

        def keys_values(k):
            keys = jnp.concatenate([b[0:tok, lanes(k)] for b in blocks], axis=0)
            values = jnp.concatenate([b[tok + META : 2 * tok + META, lanes(k)] for b in blocks], axis=0)
            return keys, values

        def body(i, _):
            base = i * HEADS_STEP
            keys, values = keys_values(lax.div(base, GROUP))
            queries = jnp.concatenate([q_ref[:, lanes(base + j)] for j in range(HEADS_STEP)], axis=0)
            scores = lax.dot_general(queries, keys, NT, preferred_element_type=jnp.float32)
            weights, totals, fades = [], [], []
            for j in range(HEADS_STEP):
                old = None if first else peak_ref[base + j]
                peak, fade, total, weight = softmax_tile(
                    scores[j * tok : (j + 1) * tok], lambda c: bias_ref[c], old
                )
                if not first:
                    total = total + total_ref[base + j] * fade
                if not last:
                    peak_ref[base + j] = peak
                    total_ref[base + j] = total
                weights.append(weight)
                totals.append(total)
                fades.append(fade)
            mixed = jnp.dot(
                jnp.concatenate(weights, axis=0), values, preferred_element_type=jnp.float32
            )
            for j in range(HEADS_STEP):
                acc = mixed[j * tok : (j + 1) * tok]
                if not first:
                    acc = acc + acc_ref[base + j] * fades[j]
                if last:
                    whole = jnp.sum(totals[j], axis=-1, keepdims=True)
                    out_ref[:, lanes(base + j)] = (acc / whole).astype(jnp.bfloat16)
                else:
                    acc_ref[base + j] = acc
            return 0

        lax.fori_loop(0, heads // HEADS_STEP, body, 0)

        def dec_body(k, _):
            keys, values = keys_values(k)
            dec_step(k, keys, values, lambda c: dbias_ref[c], False)
            return 0

        lax.fori_loop(0, hd, dec_body, 0)

    def dec_step(k, keys, values, bias, first):
        at = heads + k
        scores = lax.dot_general(
            dq_ref[tp * hd + k], keys, NT, preferred_element_type=jnp.float32
        )
        old = None if first else peak_ref[at]
        peak, fade, total, weight = softmax_tile(scores, bias, old)
        acc = jnp.dot(weight, values, preferred_element_type=jnp.float32)
        if not first:
            total = total + total_ref[at] * fade
            acc = acc + acc_ref[at] * fade
        peak_ref[at] = peak
        total_ref[at] = total
        acc_ref[at] = acc

    drow = lax.broadcasted_iota(jnp.int32, (rows * per_row, HD), 0)
    dlane = lax.broadcasted_iota(jnp.int32, (rows * per_row, HD), 1)
    steps = per_row // GROUP
    fresh_live = (lax.div(drow, per_row) == lax.div(dlane, steps)) & (
        lax.rem(dlane, steps) <= lax.rem(drow, steps)
    )
    dbias_ref[0] = jnp.where(fresh_live, 0.0, FILL)

    def fresh_body(k, _):
        dec_step(k, fresh_ref[0, :, lanes(k)], fresh_ref[1, :, lanes(k)], lambda c: dbias_ref[0], True)
        return 0

    lax.fori_loop(0, hd, fresh_body, 0)

    chunk([load_ref] + sib_arrive(0), True, False)

    crow = lax.broadcasted_iota(jnp.int32, (per_row, HD), 1)
    for r in range(rows):
        for copy in cache_copies[r]:
            copy.wait()

        def cache_body(k, _):
            queries = dq_ref[k, r * per_row : (r + 1) * per_row, :]
            scores = lax.dot_general(
                queries, ck[r, :, lanes(k)], NT, preferred_element_type=jnp.float32
            )
            limit = len_ref[r] - tp * cache_dev
            peak, _, total, weight = softmax_tile(
                scores, lambda c: jnp.where(crow + c * HD < limit, 0.0, FILL), None
            )
            acc = jnp.dot(weight, cv[r, :, lanes(k)], preferred_element_type=jnp.float32)
            whole = jnp.broadcast_to(jnp.sum(total, axis=-1, keepdims=True), total.shape)
            cst[k, 0, r * per_row : (r + 1) * per_row, :] = acc
            cst[k, 1, r * per_row : (r + 1) * per_row, :] = jnp.where(crow < HD // 2, peak, whole)
            return 0

        lax.fori_loop(0, KVH, cache_body, 0)

    def tp_copy(d):
        other = lax.rem(tp + d, n_tp)
        return pltpu.make_async_remote_copy(
            src_ref=cst.at[pl.ds(other * hd, hd)],
            dst_ref=rx.at[d],
            send_sem=tp_send.at[d],
            recv_sem=tp_recv.at[d],
            device_id={"tp": other},
            device_id_type=pl.DeviceIdType.MESH,
        )

    tp_copies = [tp_copy(d) for d in range(1, n_tp)]
    for copy in tp_copies:
        copy.start()

    arrived = ring_arrive(1)
    chunk(arrived, False, False)
    for step in range(2, half):
        arrived = ring_arrive(step)
        chunk(sib_arrive(step - 1) + arrived, False, False)
    arrived = ring_arrive(half)
    chunk(sib_arrive(half - 1), False, False)
    chunk(arrived + sib_arrive(half), False, True)

    for copy in tp_copies:
        copy.wait_recv()

    def final_body(k, _):
        at = heads + k
        peak, acc = peak_ref[at], acc_ref[at]
        whole = jnp.broadcast_to(jnp.sum(total_ref[at], axis=-1, keepdims=True), acc.shape)
        for d in range(n_tp):
            if d == 0:
                part, stats = cst[tp * hd + k, 0], cst[tp * hd + k, 1]
            else:
                part, stats = rx[d, k, 0], rx[d, k, 1]
            far_peak = jnp.broadcast_to(stats[:, 0:1], acc.shape)
            far_whole = jnp.broadcast_to(stats[:, HD // 2 : HD // 2 + 1], acc.shape)
            top = jnp.maximum(peak, far_peak)
            fade, far_fade = jnp.exp2(peak - top), jnp.exp2(far_peak - top)
            whole = whole * fade + far_whole * far_fade
            acc = acc * fade + part * far_fade
            peak = top
        dec_ref[k] = (acc / whole).astype(jnp.bfloat16)
        return 0

    lax.fori_loop(0, hd, final_body, 0)
    for copy in sent:
        copy.wait_send()
    for copy in tp_copies:
        copy.wait_send()


def per_device(
    n_ctx,
    n_tp,
    pre_queries,
    pre_keys,
    pre_values,
    block_pos,
    block_dest,
    dec_queries,
    new_keys,
    new_values,
    cache_keys,
    cache_values,
    cache_len,
):
    tok, width = pre_keys.shape
    hd = width // HD
    rows, steps = dec_queries.shape[:2]
    cache_dev = cache_keys.shape[1]
    dec_all = rows * steps * GROUP
    half = n_ctx // 4
    half_len = tok // 2

    marks = jnp.stack([jnp.repeat(block_pos, half_len), jnp.repeat(block_dest[:, 0], half_len)])
    marks = jnp.pad(marks.astype(jnp.bfloat16), ((0, META - 2), (0, width - tok)))
    load = jnp.concatenate([pre_keys, marks, pre_values], axis=0)
    dq = dec_queries.reshape(rows, steps, KVH, GROUP, HD).transpose(2, 0, 3, 1, 4)
    dq = dq.reshape(KVH, dec_all, HD)
    fresh = jnp.stack([new_keys, new_values]).reshape(2, rows * steps, width)
    fresh = jnp.pad(fresh, ((0, 0), (0, HD - rows * steps), (0, 0)))

    vmem = pl.BlockSpec(memory_space=pltpu.VMEM)
    smem = pl.BlockSpec(memory_space=pltpu.SMEM)
    hbm = pl.BlockSpec(memory_space=pl.ANY)
    states = hd * GROUP + hd
    out, dec = pl.pallas_call(
        functools.partial(kernel, n_ctx, n_tp),
        out_shape=(
            jax.ShapeDtypeStruct((tok, hd * GROUP * HD), jnp.bfloat16),
            jax.ShapeDtypeStruct((hd, dec_all, HD), jnp.bfloat16),
        ),
        in_specs=[smem, smem, vmem, vmem, vmem, vmem, hbm, hbm],
        out_specs=(vmem, vmem),
        scratch_shapes=[
            pltpu.VMEM((n_ctx, 2 * tok + META, width), jnp.bfloat16),
            pltpu.VMEM((states, tok, HD), jnp.float32),
            pltpu.VMEM((states, tok, HD), jnp.float32),
            pltpu.VMEM((states, tok, HD), jnp.float32),
            pltpu.VMEM((4, tok, HD), jnp.float32),
            pltpu.VMEM((4, dec_all, HD), jnp.float32),
            pltpu.VMEM((rows, cache_dev, KVH * HD), jnp.bfloat16),
            pltpu.VMEM((rows, cache_dev, KVH * HD), jnp.bfloat16),
            pltpu.VMEM((KVH, 2, dec_all, HD), jnp.float32),
            pltpu.VMEM((n_tp, hd, 2, dec_all, HD), jnp.float32),
            pltpu.SemaphoreType.DMA((2, half + 1)),
            pltpu.SemaphoreType.DMA((2, half + 1)),
            pltpu.SemaphoreType.DMA((2, half + 1)),
            pltpu.SemaphoreType.DMA((2, half + 1)),
            pltpu.SemaphoreType.DMA((n_tp,)),
            pltpu.SemaphoreType.DMA((n_tp,)),
            pltpu.SemaphoreType.DMA((rows, 2)),
        ],
        compiler_params=pltpu.CompilerParams(
            collective_id=0, has_side_effects=True, vmem_limit_bytes=56 * 1024 * 1024
        ),
    )(block_pos, cache_len, load, pre_queries, dq, fresh, cache_keys, cache_values)
    dec = dec.reshape(hd, rows, GROUP, steps, HD).transpose(1, 3, 0, 2, 4)
    return out, dec.reshape(rows, steps, hd * GROUP * HD)


def solution(mesh):
    placed = (
        P("ctx", "tp"),
        P("ctx", "tp"),
        P("ctx", "tp"),
        P("ctx"),
        P("ctx", None),
        P("ctx", None, None),
        P("ctx", None, "tp"),
        P("ctx", None, "tp"),
        P("ctx", "tp", None),
        P("ctx", "tp", None),
        P("ctx"),
    )
    return jax.shard_map(
        functools.partial(per_device, mesh.shape["ctx"], mesh.shape["tp"]),
        mesh=mesh,
        in_specs=placed,
        out_specs=(P("ctx", "tp"), P("ctx", None, "tp")),
        check_vma=False,
    )
```

time: 253 us -> 90.5 us (0.36)
  matrix products: 80.2 us -> 0 us
  Pallas kernels: 0 us -> 77.1 us
  waiting for transfers between devices: 45.6 us -> 0 us
  local copies, waits for them, and re-layouts: 46.2 us -> 8.62 us
  other arithmetic: 40.4 us -> 3.75 us
  blocking collectives: 24 us -> 0 us
  between operations: 14.8 us -> 0.66 us
    dot_general x12 -> x0, matrix products: 80.2 us -> none  [the longest x6 46.5 us: absorb(): jnp.einsum(form, weights.astype(jnp.bfloat16), value_block, preferred_ele...]
    pallas_call x0 -> x1, Pallas kernels: none -> 77.1 us  [per_device(): pl.pallas_call(functools.partial(kernel, n_ctx, n_tp), out_shape=(jax.Sha...]
    all_gather x3 -> x0, waiting for transfers between devices: 44.2 us -> none  [the longest x1 38.6 us: per_device(): lax.all_gather(pre_values, 'ctx', axis=0, tiled=True)]
    reduce_sum x6 -> x0, other arithmetic: 36.3 us -> none  [absorb(): totals = totals * fade_old + weights.sum(axis=-1)]
    unnamed x54 -> x1, local copies, waits for them, and re-layouts: 27.4 us -> 3.09 us
    unnamed x1 -> x0, blocking collectives: 13.7 us -> none
    all_gather x2 -> x0, blocking collectives: 10.3 us -> none  [combined_all(): pieces = jax.tree.map(lambda part: lax.all_gather(part, axis), value)]
    dynamic_slice x5 -> x0, local copies, waits for them, and re-layouts: 6.32 us -> none  [the longest x4 6.27 us: per_device(): lax.scan(one_turn, prefill_start, tuple((by_turns(stacked, turn_total) fo...]
  transfers between devices with their start and end apart: 3 -> 0, of which waited for: 2 -> 0; matrix products, arithmetic and copies ran while one was open for 16% -> 0% of each run, Pallas kernels for 0% -> 0%
where the time goes in v1:
time: 90.5 us; the launch traced here: 90.2 us
  Pallas kernels  77.1 us (85%)
  local copies, waits for them, and re-layouts  8.62 us (10%)
  other arithmetic  3.75 us (4%)
    pallas_call x1, Pallas kernels, per_device(): pl.pallas_call(functools.partial(kernel, n_ctx, n_tp), out_shape=(jax.Sha...  77.1 us
    unnamed x1, local copies, waits for them, and re-layouts  3.09 us
    reshape x2, local copies, waits for them, and re-layouts, per_device(): dec_queries.reshape(rows, steps, KVH, GROUP, HD).transpose(2, 0, 3, 1, 4)  2.17 us

profile of v1, /device:TPU:0, one launch (start us, length us, event | category | flops | bytes accessed | tf_op | source)
XLA Modules:
  0.0 90.2 jit_solution(4236887774263841387)
XLA Ops:
  0.6 0.7 convert_bitcast_fusion
  1.3 0.1 broadcast_in_dim.7
  1.4 0.1 stack_reshape.9
  1.5 0.7 convert.10
  2.1 0.1 broadcast_in_dim.6
  2.2 0.1 stack_reshape.8
  2.3 0.7 stack.14
  3.0 0.7 stack.15
  3.7 0.7 fusion.2.fresh_ref
  4.4 1.7 %pad_maximum_fusion.load_ref = bf16[272,512]{1,0:T(8,128)(2,1)} fusion(bf16[128,512]{1,0:T(8,128)(2,1)} %param.13, bf16[16,512]{1,0:T(8,128)(2,1)S(1)} %fusion.8, bf16[128,512]{1,0:T(8,128)(2,1)} %param.12), kind=kLoop, calls=%fused_computation.3 | loop fusion | flops 835584 | bytes 557056 | tf_op jit(solution)/shard_map/concatenate | solution.py:376
  6.1 1.2 %reshape.21 = bf16[2,4,8,16,128]{4,3,2,1,0:T(8,128)(2,1)S(1)} reshape(bf16[2,4,16384]{2,1,0:T(4,128)(2,1)} %param.16) | data formatting | bytes 524288 | tf_op jit(solution)/shard_map/reshape | solution.py:377
  7.4 0.9 %copy.13 = bf16[2,4,8,16,128]{4,1,3,0,2:T(4,128)(2,1)} copy(bf16[2,4,8,16,128]{4,3,2,1,0:T(8,128)(2,1)S(1)} %reshape.21) | data formatting | bytes 524288 | tf_op jit(solution)/shard_map/reshape | solution.py:377
  8.3 77.1 %shard_map.122 = (bf16[128,8192]{1,0:T(8,128)(2,1)}, bf16[4,128,128]{2,1,0:T(8,128)(2,1)}) custom-call(s32[2]{0:T(128)} %pos_ref.1, s32[2]{0:T(128)} %len_ref.1, bf16[272,512]{1,0:T(8,128)(2,1)} %pad_maximum_fusion.load_ref, bf16[128,8192]{1,0:T(8,128)(2,1)} %q_ref.1, bf16[8,128,128]{2,1,0:T(8,128)(2,1)} %bitcast.10, bf16[2,128,512]{2,1,0:T(8,128)(2,1)} %fusion.2.fresh_ref, ...), custom_call_target="tpu_custom_call" | custom-call | tf_op jit(solution)/shard_map/pallas_call | solution.py:386
  85.4 0.9 %copy.14 = bf16[2,4,4,16,128]{4,3,2,1,0:T(8,128)(2,1)S(1)} copy(bf16[2,4,4,16,128]{4,1,3,0,2:T(4,128)(2,1)} %bitcast.11) | data formatting | bytes 262144 | tf_op jit(solution)/shard_map/transpose | solution.py:417
  86.4 0.7 reshape.24
  87.1 3.1 %copy.16 = bf16[128,8192]{1,0:T(8,128)(2,1)} copy(bf16[128,8192]{1,0:T(8,128)(2,1)} %get-tuple-element.8) | data formatting | bytes 4194304
  (1 shorter events, 0.0 us)

commit v2 on v1

--- a/solution.py
+++ b/solution.py
@@ -15,7 +15,7 @@
 FILL = -1e30
 C2 = math.log2(math.e) / math.sqrt(HD)
 META = 16
-HEADS_STEP = 4
+HEADS_STEP = 8
 NT = (((1,), (1,)), ((), ()))
 
 
@@ -42,9 +42,11 @@
     n_ctx,
     n_tp,
     pos_ref,
+    dest_ref,
     len_ref,
-    load_ref,
-    q_ref,
+    k_ref,
+    v_ref,
+    q_hbm,
     dq_ref,
     fresh_ref,
     ck_hbm,
@@ -52,6 +54,7 @@
     out_ref,
     dec_ref,
     slots,
+    q_ref,
     peak_ref,
     total_ref,
     acc_ref,
@@ -68,10 +71,11 @@
     tp_send,
     tp_recv,
     cache_sem,
+    q_sem,
 ):
     tok = q_ref.shape[0]
     half_len = tok // 2
-    hd = load_ref.shape[1] // HD
+    hd = k_ref.shape[1] // HD
     heads = hd * GROUP
     rows = ck.shape[0]
     cache_dev = ck.shape[1]
@@ -99,6 +103,8 @@
 
     right, left = owner(place + 1), owner(place - 1)
 
+    q_copy = pltpu.make_async_copy(q_hbm, q_ref, q_sem)
+    q_copy.start()
     cache_copies = []
     for r in range(rows):
         pair = []
@@ -108,6 +114,17 @@
             pair.append(copy)
         cache_copies.append(pair)
 
+    slots[me, 0:tok, :] = k_ref[...]
+    slots[me, tok + META : 2 * tok + META, :] = v_ref[...]
+    mark = lax.broadcasted_iota(jnp.int32, (META, hd * HD), 0)
+    near = lax.broadcasted_iota(jnp.int32, (META, hd * HD), 1) < half_len
+    marks = jnp.where(
+        mark == 0,
+        jnp.where(near, pos_ref[0], pos_ref[1]),
+        jnp.where(near, dest_ref[0, 0], dest_ref[1, 0]),
+    )
+    slots[me, tok : tok + META, :] = marks.astype(jnp.float32).astype(jnp.bfloat16)
+
     barrier = pltpu.get_barrier_semaphore()
     for other in (right, left, sibling):
         pl.semaphore_signal(
@@ -122,63 +139,63 @@
         )
     pl.semaphore_wait(barrier, 3 + n_tp - 1)
 
-    def ring_copy(way, step, src, slot, part):
-        dst = slots.at[slot] if part is None else slots.at[slot, part]
+    pieces = (pl.ds(0, tok + META), pl.ds(tok + META, tok))
+    sent = []
+
+    def ring_copy(way, step, piece, slot):
+        ref = slots.at[slot, pieces[piece]]
         return pltpu.make_async_remote_copy(
-            src_ref=dst if src is None else src,
-            dst_ref=dst,
-            send_sem=ring_send.at[way, step],
-            recv_sem=ring_recv.at[way, step],
+            src_ref=ref,
+            dst_ref=ref,
+            send_sem=ring_send.at[way, step, piece],
+            recv_sem=ring_recv.at[way, step, piece],
             device_id={"ctx": left if way else right},
             device_id_type=pl.DeviceIdType.MESH,
         )
 
-    def sib_copy(way, step, src, slot):
-        dst = slots.at[slot]
+    def sib_copy(way, step, piece, slot):
+        ref = slots.at[slot, pieces[piece]]
         return pltpu.make_async_remote_copy(
-            src_ref=dst if src is None else src,
-            dst_ref=dst,
-            send_sem=sib_send.at[way, step],
-            recv_sem=sib_recv.at[way, step],
+            src_ref=ref,
+            dst_ref=ref,
+            send_sem=sib_send.at[way, step, piece],
+            recv_sem=sib_recv.at[way, step, piece],
             device_id={"ctx": sibling},
             device_id_type=pl.DeviceIdType.MESH,
         )
-
-    first_part, second_part = pl.ds(0, tok + META), pl.ds(tok + META, tok)
-    sent = []
 
     def start(copy):
         copy.start()
         sent.append(copy)
 
-    def part_of(way, step):
-        if step < half:
-            return None
-        return second_part if way else first_part
-
-    start(ring_copy(0, 1, load_ref, me, None))
-    start(ring_copy(1, 1, load_ref, me, None))
-    start(sib_copy(0, 0, load_ref, me))
-
-    def ring_arrive(step):
+    def ways_of(step, piece):
+        return (0, 1) if step < half else (piece,)
+
+    def arrive(step, piece):
         slot = [owner(place - step), owner(place + step)]
-        for way in (0, 1):
-            ring_copy(way, step, None, slot[way], part_of(way, step)).wait_recv()
-            if step < half:
-                start(ring_copy(way, step + 1, None, slot[way], part_of(way, step + 1)))
-        if step < half:
-            start(sib_copy(0, step, None, slot[0]))
-            start(sib_copy(1, step, None, slot[1]))
-            return [slots.at[slot[0]], slots.at[slot[1]]]
-        start(sib_copy(0, step, None, slot[0]))
-        return [slots.at[slot[0]]]
+        for way in ways_of(step, piece):
+            ring_copy(way, step, piece, slot[way]).wait_recv()
+            if step < half and way in ways_of(step + 1, piece):
+                start(ring_copy(way, step + 1, piece, slot[way]))
+            start(sib_copy(way, step, piece, slot[way]))
 
     def sib_arrive(step):
         slot = [sib_owner(place - step), sib_owner(place + step)]
-        ways = (0, 1) if 0 < step < half else (0,)
-        for way in ways:
-            sib_copy(way, step, None, slot[way]).wait_recv()
-        return [slots.at[slot[way]] for way in ways]
+        for piece in (0, 1):
+            for way in ways_of(step, piece) if step else (0,):
+                sib_copy(way, step, piece, slot[way]).wait_recv()
+
+    def blocks_of(step):
+        if step == 0:
+            return [slots.at[me], slots.at[sibling]]
+        if step == half:
+            return [slots.at[owner(place + step)], slots.at[sib_owner(place + step)]]
+        return [slots.at[o(place + way * step)] for o in (owner, sib_owner) for way in (-1, 1)]
+
+    for piece in (0, 1):
+        start(ring_copy(0, 1, piece, me))
+        start(ring_copy(1, 1, piece, me))
+        start(sib_copy(0, 0, piece, me))
 
     row = lax.broadcasted_iota(jnp.int32, (tok, HD), 0)
     lane = lax.broadcasted_iota(jnp.int32, (tok, HD), 1)
@@ -187,8 +204,9 @@
     lane_off = lax.rem(lane, half_len).astype(jnp.float32)
     me_f = me.astype(jnp.float32)
 
-    def chunk(blocks, first, last):
-        width = len(blocks)
+    def chunk(step, between):
+        first, last = step == 0, step == half
+        blocks = blocks_of(step)
         for c, block in enumerate(blocks):
             meta = block[tok : tok + META, 0:HD].astype(jnp.float32)
             key_pos = meta[0:1, :] * float(half_len) + lane_off
@@ -233,14 +251,20 @@
                     acc_ref[base + j] = acc
             return 0
 
-        lax.fori_loop(0, heads // HEADS_STEP, body, 0)
+        turns = heads // HEADS_STEP
+        if between is None:
+            lax.fori_loop(0, turns, body, 0)
+        else:
+            lax.fori_loop(0, turns // 2, body, 0)
+            between()
+            lax.fori_loop(turns // 2, turns, body, 0)
 
         def dec_body(k, _):
             keys, values = keys_values(k)
             dec_step(k, keys, values, lambda c: dbias_ref[c], False)
             return 0
 
-        lax.fori_loop(0, hd, dec_body, 0)
+        lax.fori_loop(0, hd, dec_body, 0, unroll=True)
 
     def dec_step(k, keys, values, bias, first):
         at = heads + k
@@ -269,19 +293,23 @@
         dec_step(k, fresh_ref[0, :, lanes(k)], fresh_ref[1, :, lanes(k)], lambda c: dbias_ref[0], True)
         return 0
 
-    lax.fori_loop(0, hd, fresh_body, 0)
-
-    chunk([load_ref] + sib_arrive(0), True, False)
+    lax.fori_loop(0, hd, fresh_body, 0, unroll=True)
+
+    q_copy.wait()
+    sib_arrive(0)
+    chunk(0, None)
+    arrive(1, 0)
 
     crow = lax.broadcasted_iota(jnp.int32, (per_row, HD), 1)
-    for r in range(rows):
-        for copy in cache_copies[r]:
+    for pair in cache_copies:
+        for copy in pair:
             copy.wait()
 
-        def cache_body(k, _):
-            queries = dq_ref[k, r * per_row : (r + 1) * per_row, :]
+    def cache_body(k, _):
+        for r in range(rows):
+            span = slice(r * per_row, (r + 1) * per_row)
             scores = lax.dot_general(
-                queries, ck[r, :, lanes(k)], NT, preferred_element_type=jnp.float32
+                dq_ref[k, span, :], ck[r, :, lanes(k)], NT, preferred_element_type=jnp.float32
             )
             limit = len_ref[r] - tp * cache_dev
             peak, _, total, weight = softmax_tile(
@@ -289,11 +317,13 @@
             )
             acc = jnp.dot(weight, cv[r, :, lanes(k)], preferred_element_type=jnp.float32)
             whole = jnp.broadcast_to(jnp.sum(total, axis=-1, keepdims=True), total.shape)
-            cst[k, 0, r * per_row : (r + 1) * per_row, :] = acc
-            cst[k, 1, r * per_row : (r + 1) * per_row, :] = jnp.where(crow < HD // 2, peak, whole)
-            return 0
-
-        lax.fori_loop(0, KVH, cache_body, 0)
+            cst[k, 0, span, :] = acc
+            cst[k, 1, span, :] = jnp.where(crow < HD // 2, peak, whole)
+        return 0
+
+    lax.fori_loop(0, KVH // 2, cache_body, 0)
+    arrive(1, 1)
+    lax.fori_loop(KVH // 2, KVH, cache_body, 0)
 
     def tp_copy(d):
         other = lax.rem(tp + d, n_tp)
@@ -310,14 +340,19 @@
     for copy in tp_copies:
         copy.start()
 
-    arrived = ring_arrive(1)
-    chunk(arrived, False, False)
-    for step in range(2, half):
-        arrived = ring_arrive(step)
-        chunk(sib_arrive(step - 1) + arrived, False, False)
-    arrived = ring_arrive(half)
-    chunk(sib_arrive(half - 1), False, False)
-    chunk(arrived + sib_arrive(half), False, True)
+    for step in range(1, half):
+        sib_arrive(step)
+
+        def between():
+            arrive(step + 1, 0)
+            if step + 1 == half:
+                arrive(half, 1)
+
+        chunk(step, between)
+        if step + 1 < half:
+            arrive(step + 1, 1)
+    sib_arrive(half)
+    chunk(half, None)
 
     for copy in tp_copies:
         copy.wait_recv()
@@ -341,7 +376,7 @@
         dec_ref[k] = (acc / whole).astype(jnp.bfloat16)
         return 0
 
-    lax.fori_loop(0, hd, final_body, 0)
+    lax.fori_loop(0, hd, final_body, 0, unroll=True)
     for copy in sent:
         copy.wait_send()
     for copy in tp_copies:
@@ -369,11 +404,7 @@
     cache_dev = cache_keys.shape[1]
     dec_all = rows * steps * GROUP
     half = n_ctx // 4
-    half_len = tok // 2
-
-    marks = jnp.stack([jnp.repeat(block_pos, half_len), jnp.repeat(block_dest[:, 0], half_len)])
-    marks = jnp.pad(marks.astype(jnp.bfloat16), ((0, META - 2), (0, width - tok)))
-    load = jnp.concatenate([pre_keys, marks, pre_values], axis=0)
+
     dq = dec_queries.reshape(rows, steps, KVH, GROUP, HD).transpose(2, 0, 3, 1, 4)
     dq = dq.reshape(KVH, dec_all, HD)
     fresh = jnp.stack([new_keys, new_values]).reshape(2, rows * steps, width)
@@ -389,10 +420,11 @@
             jax.ShapeDtypeStruct((tok, hd * GROUP * HD), jnp.bfloat16),
             jax.ShapeDtypeStruct((hd, dec_all, HD), jnp.bfloat16),
         ),
-        in_specs=[smem, smem, vmem, vmem, vmem, vmem, hbm, hbm],
+        in_specs=[smem, smem, smem, vmem, vmem, hbm, vmem, vmem, hbm, hbm],
         out_specs=(vmem, vmem),
         scratch_shapes=[
             pltpu.VMEM((n_ctx, 2 * tok + META, width), jnp.bfloat16),
+            pltpu.VMEM(pre_queries.shape, jnp.bfloat16),
             pltpu.VMEM((states, tok, HD), jnp.float32),
             pltpu.VMEM((states, tok, HD), jnp.float32),
             pltpu.VMEM((states, tok, HD), jnp.float32),
@@ -402,18 +434,30 @@
             pltpu.VMEM((rows, cache_dev, KVH * HD), jnp.bfloat16),
             pltpu.VMEM((KVH, 2, dec_all, HD), jnp.float32),
             pltpu.VMEM((n_tp, hd, 2, dec_all, HD), jnp.float32),
-            pltpu.SemaphoreType.DMA((2, half + 1)),
-            pltpu.SemaphoreType.DMA((2, half + 1)),
-            pltpu.SemaphoreType.DMA((2, half + 1)),
-            pltpu.SemaphoreType.DMA((2, half + 1)),
+            pltpu.SemaphoreType.DMA((2, half + 1, 2)),
+            pltpu.SemaphoreType.DMA((2, half + 1, 2)),
+            pltpu.SemaphoreType.DMA((2, half + 1, 2)),
+            pltpu.SemaphoreType.DMA((2, half + 1, 2)),
             pltpu.SemaphoreType.DMA((n_tp,)),
             pltpu.SemaphoreType.DMA((n_tp,)),
             pltpu.SemaphoreType.DMA((rows, 2)),
+            pltpu.SemaphoreType.DMA,
         ],
         compiler_params=pltpu.CompilerParams(
             collective_id=0, has_side_effects=True, vmem_limit_bytes=56 * 1024 * 1024
         ),
-    )(block_pos, cache_len, load, pre_queries, dq, fresh, cache_keys, cache_values)
+    )(
+        block_pos,
+        block_dest,
+        cache_len,
+        pre_keys,
+        pre_values,
+        pre_queries,
+        dq,
+        fresh,
+        cache_keys,
+        cache_values,
+    )
     dec = dec.reshape(hd, rows, GROUP, steps, HD).transpose(1, 3, 0, 2, 4)
     return out, dec.reshape(rows, steps, hd * GROUP * HD)
 

time: 90.5 us -> 67.1 us (0.74)
  Pallas kernels: 77.1 us -> 55.8 us
  other arithmetic: 3.75 us -> 0.76 us
  local copies, waits for them, and re-layouts: 8.62 us -> 9.56 us
    pallas_call x1, Pallas kernels: 77.1 us -> 55.8 us  [per_device(): pl.pallas_call(functools.partial(kernel, n_ctx, n_tp), out_shape=(jax.Sha...]
    concatenate x1 -> x0, other arithmetic: 1.69 us -> none  [per_device(): load = jnp.concatenate([pre_keys, marks, pre_values], axis=0)]
    another operation x3 -> x0, other arithmetic: 1.33 us -> none
    unnamed x1 -> x2, local copies, waits for them, and re-layouts: 3.09 us -> 4.39 us
where the time goes in v2:
time: 67.1 us; the launch traced here: 66.8 us
  Pallas kernels  55.8 us (83%)
  local copies, waits for them, and re-layouts  9.56 us (14%)
  other arithmetic  0.76 us (1%)
    pallas_call x1, Pallas kernels, per_device(): pl.pallas_call(functools.partial(kernel, n_ctx, n_tp), out_shape=(jax.Sha...  55.8 us
    unnamed x2, local copies, waits for them, and re-layouts  4.39 us
    reshape x2, local copies, waits for them, and re-layouts, per_device(): dec_queries.reshape(rows, steps, KVH, GROUP, HD).transpose(2, 0, 3, 1, 4)  2.14 us
    another operation x2, local copies, waits for them, and re-layouts, per_device(): fresh = jnp.stack([new_keys, new_values]).reshape(2, rows * steps, width)  1.41 us

profile of v2, /device:TPU:0, one launch (start us, length us, event | category | flops | bytes accessed | tf_op | source)
XLA Modules:
  0.0 66.8 jit_solution(17032475266183560006)
XLA Ops:
  0.6 1.3 %copy.14.dest_ref = s32[2,1]{1,0:T(2,128)} copy(s32[2,1]{0,1:T(1,128)} %param.15) | data formatting | bytes 16 | tf_op args[4]
  1.9 0.7 %stack.9 = bf16[1,8,512]{2,1,0:T(8,128)(2,1)S(1)} reshape(bf16[2,4,512]{2,1,0:T(4,128)(2,1)} %param.17) | data formatting | bytes 16384 | tf_op jit(solution)/shard_map/stack | solution.py:410
  2.6 0.7 %stack.10 = bf16[1,8,512]{2,1,0:T(8,128)(2,1)S(1)} reshape(bf16[2,4,512]{2,1,0:T(4,128)(2,1)} %param.18) | data formatting | bytes 16384 | tf_op jit(solution)/shard_map/stack | solution.py:410
  3.3 0.8 %fusion.2.fresh_ref = bf16[2,128,512]{2,1,0:T(8,128)(2,1)} fusion(bf16[1,8,512]{2,1,0:T(8,128)(2,1)S(1)} %stack.10, bf16[1,8,512]{2,1,0:T(8,128)(2,1)S(1)} %stack.9), kind=kLoop, calls=%fused_computation.3 | loop fusion | flops 917504 | bytes 278528 | tf_op jit(solution)/shard_map/stack | solution.py:410
  4.1 1.2 %reshape.21 = bf16[2,4,8,16,128]{4,3,2,1,0:T(8,128)(2,1)S(1)} reshape(bf16[2,4,16384]{2,1,0:T(4,128)(2,1)} %param.16) | data formatting | bytes 524288 | tf_op jit(solution)/shard_map/reshape | solution.py:408
  5.3 0.9 %copy.13 = bf16[2,4,8,16,128]{4,1,3,0,2:T(4,128)(2,1)} copy(bf16[2,4,8,16,128]{4,3,2,1,0:T(8,128)(2,1)S(1)} %reshape.21) | data formatting | bytes 524288 | tf_op jit(solution)/shard_map/reshape | solution.py:408
  6.2 55.8 %shard_map.122 = (bf16[128,8192]{1,0:T(8,128)(2,1)}, bf16[4,128,128]{2,1,0:T(8,128)(2,1)}) custom-call(s32[2]{0:T(128)} %pos_ref.1, s32[2,1]{1,0:T(2,128)} %copy.14.dest_ref, s32[2]{0:T(128)} %len_ref.1, bf16[128,512]{1,0:T(8,128)(2,1)} %k_ref.1, bf16[128,512]{1,0:T(8,128)(2,1)} %v_ref.1, bf16[128,8192]{1,0:T(8,128)(2,1)} %q_hbm.1, ...), custom_call_target="tpu_custom_call" | custom-call | tf_op jit(solution)/shard_map/pallas_call | solution.py:417
  62.1 0.9 %copy.15 = bf16[2,4,4,16,128]{4,3,2,1,0:T(8,128)(2,1)S(1)} copy(bf16[2,4,4,16,128]{4,1,3,0,2:T(4,128)(2,1)} %bitcast.9) | data formatting | bytes 262144 | tf_op jit(solution)/shard_map/transpose | solution.py:461
  63.0 0.7 %reshape.24 = bf16[2,4,8192]{2,1,0:T(4,128)(2,1)} reshape(bf16[2,4,4,16,128]{4,3,2,1,0:T(8,128)(2,1)S(1)} %copy.15) | data formatting | bytes 262144 | tf_op jit(solution)/shard_map/reshape | solution.py:462
  63.7 3.1 %copy.17 = bf16[128,8192]{1,0:T(8,128)(2,1)} copy(bf16[128,8192]{1,0:T(8,128)(2,1)} %get-tuple-element.8) | data formatting | bytes 4194304
